TPU v7x, 1024 devices: a whole 4x4x32 slice. The times are simulated.
1024 devices in a mesh: grp: 8 (over x, core), nbr: 128 (over z, y).
Axes of the slice: x: 4, y: 4, z: 32, core: 2. Of those that a mesh axis runs over, the one named last changes fastest.
Arguments:
- multipole: bfloat16 [488, 262144], P(None, ('grp', 'nbr')), may hold values from -6 to 6
- dest: int32 [262144, 1], P(('grp', 'nbr')), may hold values from 0 to 7; in each aligned block of 256 rows (0 to 255, 256 to 511, ...) at most 64 rows name the same one
- parent_local: bfloat16 [488, 32768], P(None, ('grp', 'nbr')), may hold values from -6 to 6
- parent_of: int32 [524288], P(('grp', 'nbr')), may hold values from 0 to 255
- send_list: int32 [2, 262144], P(None, ('grp', 'nbr')), may hold values from 0 to 511, as said below
- lists: int32 [8, 524288], P(None, ('grp', 'nbr')), may hold values from -1 to 1023, as said below
- m2l_ops: bfloat16 [8, 488, 488], replicated, may hold values from -0.25 to 0.25
- l2l_ops: bfloat16 [8, 488, 488], replicated, may hold values from -0.25 to 0.25
Outputs:
- local_exp: float32 [488, 524288], P(None, ('grp', 'nbr'))
Inputs may be any that keep to these rules, and one draw needn't show every extreme that they name: `dest`: no leaf owner sends more than 64 boxes to one owner, and some leaf owner sends exactly 64. `send_list`: each owner's two rows together list each of its 512 slots once. `lists`: -1 marks padding.
All inputs are finite; a program needn't handle non-finite values.
Results may differ from a plain program's by a relative error of at most 0.0003.
Values may be sent and summed in bfloat16 or wider, within the bound.
A program may use at most 32 MiB of HBM per device.

v0:
```python
import jax
import jax.numpy as jnp
from jax import lax
from jax.sharding import PartitionSpec as P


def extended(cells, sides, width):
    for axis, dim in sides:
        count = lax.axis_size(axis)
        ends = count - 1
        head = lax.slice_in_dim(cells, 0, width, axis=dim)
        tail = lax.slice_in_dim(cells, cells.shape[dim] - width, cells.shape[dim], axis=dim)
        cells = jnp.concatenate(
            [
                lax.ppermute(tail, axis, [(i, (i + 1) % count) for i in range(ends)]),
                cells,
                lax.ppermute(head, axis, [((i + 1) % count, i) for i in range(ends)]),
            ],
            axis=dim,
        )
    return cells


def body(multipole, dest, parent_local, parent_of, send_list, lists, m2l_ops, l2l_ops):
    coef_count = multipole.shape[0]
    groups = lax.axis_size("grp")
    slot_count = lists.shape[1]
    capacity = slot_count // groups
    rim_count = send_list.shape[1]
    parents = parent_local.shape[1]
    target = dest[:, 0]
    onehot = (target[:, None] == jnp.arange(groups, dtype=jnp.int32)[None, :]).astype(jnp.int32)
    arrival = jnp.sum((jnp.cumsum(onehot, axis=0) - 1) * onehot, axis=1)
    position = target * capacity + arrival
    placing = (position[:, None] == jnp.arange(slot_count, dtype=jnp.int32)[None, :]).astype(
        jnp.bfloat16
    )
    outgoing = jnp.dot(multipole, placing, preferred_element_type=jnp.float32).astype(jnp.bfloat16)
    owned_coef = lax.all_to_all(
        outgoing.reshape(coef_count, groups, capacity),
        "grp",
        split_axis=1,
        concat_axis=1,
        tiled=True,
    )
    owned_coef = owned_coef.reshape(coef_count, slot_count)
    widened = extended(owned_coef, (("nbr", 1),), slot_count)
    neighbor_ids = extended(send_list, (("nbr", 1),), rim_count)
    from_left = jnp.take(widened[:, :slot_count], neighbor_ids[0, :rim_count], axis=1)
    from_right = jnp.take(widened[:, 2 * slot_count :], neighbor_ids[1, 2 * rim_count :], axis=1)
    translated = jnp.einsum(
        "okj,jp->kop", l2l_ops, parent_local, preferred_element_type=jnp.float32
    )
    translated = translated.reshape(coef_count, 8 * parents)
    accum_local = jnp.take(translated, parent_of, axis=1)
    sources = jnp.concatenate([owned_coef, from_left, from_right], axis=1)
    for offset in range(m2l_ops.shape[0]):
        entries = lists[offset]
        columns = jnp.take(sources, jnp.maximum(entries, 0), axis=1)
        columns = jnp.where((entries >= 0)[None, :], columns, jnp.zeros_like(columns))
        accum_local = accum_local + jnp.dot(
            m2l_ops[offset], columns, preferred_element_type=jnp.float32
        )
    return accum_local


def solution(mesh):
    placed = (
        P(None, ("grp", "nbr")),
        P(("grp", "nbr"), None),
        P(None, ("grp", "nbr")),
        P(("grp", "nbr")),
        P(None, ("grp", "nbr")),
        P(None, ("grp", "nbr")),
        P(),
        P(),
    )
    return jax.shard_map(
        body, mesh=mesh, in_specs=placed, out_specs=P(None, ("grp", "nbr")), check_vma=False
    )
```

profile of v0, /device:TPU:10, one launch (start us, length us, event | category | flops | bytes accessed | tf_op | source)
XLA Modules:
  0.0 83.6 jit_solution(13829448075948491953)
XLA Ops:
  0.0 0.0 copy-start
  0.0 2.5 %collective-permute-start.3 = (s32[2,256]{1,0:T(2,128)}, s32[2,256]{1,0:T(2,128)S(1)}, u32[]{:S(2)}, u32[]{:S(2)}) collective-permute-start(s32[2,256]{1,0:T(2,128)} %param.16), channel_id=1, source_target_pairs={{1,0},{2,1},{3,2},{4,3},{5,4},{6,5},{7,6},{8,7},{9,8},{10,9},{11,1... | collective-permute-start | bytes 6152 | tf_op jit(solution)/shard_map/ppermute | solution.py:17
  2.5 3.5 %collective-permute-start.1 = (s32[2,256]{1,0:T(2,128)}, s32[2,256]{1,0:T(2,128)S(1)}, u32[]{:S(2)}, u32[]{:S(2)}) collective-permute-start(s32[2,256]{1,0:T(2,128)} %param.16), channel_id=1, source_target_pairs={{0,1},{1,2},{2,3},{3,4},{4,5},{5,6},{6,7},{7,8},{8,9},{9,10},{10,1... | collective-permute-start | bytes 6152 | tf_op jit(solution)/shard_map/ppermute | solution.py:15
  6.0 0.7 fusion.64
  6.7 0.6 reduce-window.6
  7.2 0.2 slice_reduce_fusion
  7.5 0.8 fusion.63
  8.3 0.7 multiply_add_fusion
  8.9 0.0 copy-done
  9.0 0.4 fusion.3
  9.4 1.0 %copy.12 = bf16[488,512]{0,1:T(8,128)(2,1)} copy(bf16[488,512]{1,0:T(8,128)(2,1)S(1)} %fusion.3) | data formatting | bytes 999424 | tf_op jit(solution)/shard_map/convert_element_type | solution.py:38
  10.4 15.0 %all-to-all-start = ((bf16[488,8,64]{0,2,1:T(8,128)(2,1)}), bf16[488,8,64]{0,2,1:T(8,128)(2,1)S(1)}, u32[]{:S(2)}, u32[]{:S(2)}) async-start(bf16[488,8,64]{0,2,1:T(8,128)(2,1)} %bitcast.11), calls=%async_computation | async-start | bytes 1048576 | tf_op jit(solution)/shard_map/all_to_all | solution.py:39
  25.4 0.7 compare_select_fusion.8
  26.1 1.0 %slice_maximum_fusion = (s32[1,512]{1,0:T(1,128)S(1)}, s32[1,512]{1,0:T(1,128)S(1)}, s32[1,512]{1,0:T(1,128)S(1)}, s32[1,512]{1,0:T(1,128)S(1)}, s32[1,512]{1,0:...) fusion(s32[8,512]{1,0:T(8,128)} %param.17), kind=kLoop, calls=%fused_computation.142 | loop fusion | flops 4096 | bytes 32768 | tf_op jit(solution)/shard_map/max | solution.py:59
  27.1 0.7 compare_and_fusion.7
  27.8 1.1 %compare_reduce_fusion = (pred[512]{0:T(512)(128)(4,1)S(1)}, pred[512]{0:T(512)(128)(4,1)S(1)}, pred[512]{0:T(512)(128)(4,1)S(1)}, pred[512]{0:T(512)(128)(4,1)S...) fusion(s32[8,512]{1,0:T(8,128)} %param.17), kind=kLoop, calls=%fused_computation.101 | loop fusion | flops 4096 | bytes 20480 | tf_op jit(solution)/shard_map/ge | solution.py:60
  29.2 3.3 %fusion.61 = f32[32,8,488]{2,0,1:T(8,128)S(1)} fusion(bf16[8,488,488]{2,1,0:T(8,128)(2,1)} %param.19, bf16[488,32]{0,1:T(8,128)(2,1)} %param.14), kind=kOutput, calls=%fused_computation.93 | convolution fusion | flops 121929728 | bytes 4341248 | tf_op jit(solution)/shard_map/okj,jp->kop/dot_general | solution.py:51
  32.5 1.6 %gather_fusion = f32[512,488]{1,0:T(8,128)S(1)} fusion(f32[488,256]{0,1:T(8,128)S(1)} %bitcast.94, s32[1024]{0:T(1024)S(1)} %pad_clamp_fusion.10), kind=kCustom, calls=%fused_computation.10 | custom fusion | bytes 2000896 | tf_op jit(solution)/shard_map/jit(_take)/gather | solution.py:55
  34.2 1.3 %copy.11 = f32[512,488]{0,1:T(8,128)} copy(f32[512,488]{1,0:T(8,128)S(1)} %gather_fusion) | data formatting | bytes 1998848 | tf_op jit(solution)/shard_map/jit(_take)/gather | solution.py:55
  35.5 0.0 collective-permute-done.3
  35.5 0.0 collective-permute-done.1
  35.5 0.0 all-to-all-done
  35.5 3.9 %collective-permute-start.2 = (bf16[488,512]{0,1:T(8,128)(2,1)S(1)}, bf16[488,512]{0,1:T(8,128)(2,1)S(1)}, u32[]{:S(2)}, u32[]{:S(2)}) collective-permute-start(bf16[488,512]{0,1:T(8,128)(2,1)S(1)} %bitcast.95), channel_id=1, source_target_pairs={{1,0},{2,1},{3,2},{4,3},{5,4},{6,5},{7,6},{8,7},{9,8},{10,9},{11,1... | collective-permute-start | bytes 1499144 | tf_op jit(solution)/shard_map/ppermute | solution.py:17
  39.5 2.1 %collective-permute-start = (bf16[488,512]{0,1:T(8,128)(2,1)S(1)}, bf16[488,512]{0,1:T(8,128)(2,1)S(1)}, u32[]{:S(2)}, u32[]{:S(2)}) collective-permute-start(bf16[488,512]{0,1:T(8,128)(2,1)S(1)} %bitcast.96), channel_id=1, source_target_pairs={{0,1},{1,2},{2,3},{3,4},{4,5},{5,6},{6,7},{7,8},{8,9},{9,10},{10,1... | collective-permute-start | bytes 1499144 | tf_op jit(solution)/shard_map/ppermute | solution.py:15
  41.6 9.8 %collective-permute-done.2 = bf16[488,512]{0,1:T(8,128)(2,1)S(1)} collective-permute-done((bf16[488,512]{0,1:T(8,128)(2,1)S(1)}, bf16[488,512]{0,1:T(8,128)(2,1)S(1)}, u32[]{:S(2)}, u32[]{:S(2)}) %collective-permute-start.2) | collective-permute-done | bytes 499744 | tf_op jit(solution)/shard_map/ppermute | solution.py:17
  51.4 1.2 %gather_fusion.2 = bf16[256,488]{1,0:T(8,128)(2,1)S(1)} fusion(bf16[488,512]{0,1:T(8,128)(2,1)S(1)} %collective-permute-done.2, s32[1024]{0:T(1024)S(1)} %pad_clamp_fusion.8), kind=kCustom, calls=%fused_computation.2.clone | custom fusion | bytes 500736 | tf_op jit(solution)/shard_map/jit(_take)/gather | solution.py:50
  52.5 0.1 select_bitcast_fusion
  52.6 2.4 %collective-permute-done = bf16[488,512]{0,1:T(8,128)(2,1)S(1)} collective-permute-done((bf16[488,512]{0,1:T(8,128)(2,1)S(1)}, bf16[488,512]{0,1:T(8,128)(2,1)S(1)}, u32[]{:S(2)}, u32[]{:S(2)}) %collective-permute-start) | collective-permute-done | bytes 499744 | tf_op jit(solution)/shard_map/ppermute | solution.py:15
  55.0 1.2 %gather_fusion.1 = bf16[256,488]{1,0:T(8,128)(2,1)S(1)} fusion(bf16[488,512]{0,1:T(8,128)(2,1)S(1)} %collective-permute-done, s32[1024]{0:T(1024)S(1)} %pad_clamp_fusion.9), kind=kCustom, calls=%fused_computation.clone | custom fusion | bytes 500736 | tf_op jit(solution)/shard_map/jit(_take)/gather | solution.py:49
  56.2 0.1 select_bitcast_fusion.1
  56.3 0.1 pad_maximum_fusion
  56.5 2.6 %gather_fusion.3 = bf16[512,488]{1,0:T(8,128)(2,1)} fusion(bf16[488,1024]{0,1:T(8,128)(2,1)S(1)} %pad_maximum_fusion, s32[1024]{0:T(1024)S(1)} %pad_clamp_fusion.7), kind=kCustom, calls=%fused_computation.1.clone | custom fusion | bytes 1001472 | tf_op jit(solution)/shard_map/jit(_take)/gather | solution.py:59
  59.1 2.6 %gather_fusion.4 = bf16[512,488]{1,0:T(8,128)(2,1)} fusion(bf16[488,1024]{0,1:T(8,128)(2,1)S(1)} %pad_maximum_fusion, s32[1024]{0:T(1024)S(1)} %pad_clamp_fusion.6), kind=kCustom, calls=%fused_computation.3.clone | custom fusion | bytes 1001472 | tf_op jit(solution)/shard_map/jit(_take)/gather | solution.py:59
  61.7 2.6 %gather_fusion.5 = bf16[512,488]{1,0:T(8,128)(2,1)} fusion(bf16[488,1024]{0,1:T(8,128)(2,1)S(1)} %pad_maximum_fusion, s32[1024]{0:T(1024)S(1)} %pad_clamp_fusion.5), kind=kCustom, calls=%fused_computation.4.clone | custom fusion | bytes 1001472 | tf_op jit(solution)/shard_map/jit(_take)/gather | solution.py:59
  64.3 2.6 %gather_fusion.6 = bf16[512,488]{1,0:T(8,128)(2,1)} fusion(bf16[488,1024]{0,1:T(8,128)(2,1)S(1)} %pad_maximum_fusion, s32[1024]{0:T(1024)S(1)} %pad_clamp_fusion.4), kind=kCustom, calls=%fused_computation.5.clone | custom fusion | bytes 1001472 | tf_op jit(solution)/shard_map/jit(_take)/gather | solution.py:59
  67.0 2.0 %gather_fusion.7 = bf16[512,488]{1,0:T(8,128)(2,1)S(1)} fusion(bf16[488,1024]{0,1:T(8,128)(2,1)S(1)} %pad_maximum_fusion, s32[1024]{0:T(1024)S(1)} %pad_clamp_fusion.3), kind=kCustom, calls=%fused_computation.6.clone | custom fusion | bytes 1001472 | tf_op jit(solution)/shard_map/jit(_take)/gather | solution.py:59
  68.9 2.0 %gather_fusion.8 = bf16[512,488]{1,0:T(8,128)(2,1)S(1)} fusion(bf16[488,1024]{0,1:T(8,128)(2,1)S(1)} %pad_maximum_fusion, s32[1024]{0:T(1024)S(1)} %pad_clamp_fusion.2), kind=kCustom, calls=%fused_computation.7.clone | custom fusion | bytes 1001472 | tf_op jit(solution)/shard_map/jit(_take)/gather | solution.py:59
  70.9 2.0 %gather_fusion.9 = bf16[512,488]{1,0:T(8,128)(2,1)S(1)} fusion(bf16[488,1024]{0,1:T(8,128)(2,1)S(1)} %pad_maximum_fusion, s32[1024]{0:T(1024)S(1)} %pad_clamp_fusion.1), kind=kCustom, calls=%fused_computation.8.clone | custom fusion | bytes 1001472 | tf_op jit(solution)/shard_map/jit(_take)/gather | solution.py:59
  72.9 2.0 %gather_fusion.10 = bf16[512,488]{1,0:T(8,128)(2,1)S(1)} fusion(bf16[488,1024]{0,1:T(8,128)(2,1)S(1)} %pad_maximum_fusion, s32[1024]{0:T(1024)S(1)} %pad_clamp_fusion), kind=kCustom, calls=%fused_computation.9.clone | custom fusion | bytes 1001472 | tf_op jit(solution)/shard_map/jit(_take)/gather | solution.py:59
  74.9 0.0 copy-start.1
  74.9 0.0 copy-start.3
  74.9 0.0 copy-start.2
  74.9 2.3 %convolution_add_fusion.5 = f32[512,488]{0,1:T(8,128)S(1)} fusion(f32[512,488]{0,1:T(8,128)} %copy.11, bf16[512,488]{1,0:T(8,128)(2,1)} %gather_fusion.3, pred[512]{0:T(512)(128)(4,1)S(1)} %get-tuple-element.23, pred[512]{0:T(512)(128)(4,1)S(1)} %get-tuple-element.13, bf16[8,488,488]{2,1,0:T(8,128)(2,1)} %param.18, pred[512]{0:T(512)(128)(4,1)S(1)} %get-tuple-element.24), kind=kOutput, calls=%fused_computation.21 | convolution fusion | flops 244858880 | bytes 3024384 | tf_op jit(solution)/shard_map/dot_general | solution.py:61
  77.2 1.8 %convolution_add_fusion.4 = f32[512,488]{0,1:T(8,128)S(1)} fusion(f32[512,488]{0,1:T(8,128)S(1)} %convolution_add_fusion.5, bf16[512,488]{1,0:T(8,128)(2,1)} %gather_fusion.4, pred[512]{0:T(512)(128)(4,1)S(1)} %compare_and_fusion.6, pred[512]{0:T(512)(128)(4,1)S(1)} %get-tuple-element.12, bf16[8,488,488]{2,1,0:T(8,128)(2,1)} %param.18), kind=kOutput, calls=%fused_computation.20 | convolution fusion | flops 244609024 | bytes 3023872 | tf_op jit(solution)/shard_map/dot_general | solution.py:61
  79.0 0.0 copy-done.1
  79.0 0.0 copy-done.3
  79.0 0.6 convolution_add_fusion.3
  79.6 0.0 copy-done.2
  79.6 0.6 convolution_add_fusion.2
  80.2 0.6 convolution_add_fusion.1
  80.9 0.6 fusion.2
  81.5 0.6 fusion.1
  82.1 1.6 %fusion = f32[488,512]{1,0:T(8,128)} fusion(f32[488,512]{1,0:T(8,128)S(1)} %fusion.1, bf16[512,488]{1,0:T(8,128)(2,1)S(1)} %gather_fusion.10, pred[512]{0:T(512)(128)(4,1)S(1)} %compare_and_fusion, pred[512]{0:T(512)(128)(4,1)S(1)} %get-tuple-element.6, bf16[8,488,488]{2,1,0:T(8,128)(2,1)S(1)} %copy-done.1), kind=kOutput, calls=%fused_computation.12 | convolution fusion | flops 244609024 | bytes 3023872 | tf_op jit(solution)/shard_map/dot_general | solution.py:61
  (34 shorter events, 0.2 us)
Async XLA Ops:
  0.0 8.9 %copy-start = (bf16[488,256]{1,0:T(8,128)(2,1)S(1)}, bf16[488,256]{1,0:T(8,128)(2,1)}, u32[]{:S(2)}) copy-start(bf16[488,256]{1,0:T(8,128)(2,1)} %param.12) | copy-start | bytes 749572
  0.0 35.4 %collective-permute-start.3 = (s32[2,256]{1,0:T(2,128)}, s32[2,256]{1,0:T(2,128)S(1)}, u32[]{:S(2)}, u32[]{:S(2)}) collective-permute-start(s32[2,256]{1,0:T(2,128)} %param.16), channel_id=1, source_target_pairs={{1,0},{2,1},{3,2},{4,3},{5,4},{6,5},{7,6},{8,7},{9,8},{10,9},{11,1... | collective-permute-start | bytes 6152 | tf_op jit(solution)/shard_map/ppermute | solution.py:17
  2.5 33.0 %collective-permute-start.1 = (s32[2,256]{1,0:T(2,128)}, s32[2,256]{1,0:T(2,128)S(1)}, u32[]{:S(2)}, u32[]{:S(2)}) collective-permute-start(s32[2,256]{1,0:T(2,128)} %param.16), channel_id=1, source_target_pairs={{0,1},{1,2},{2,3},{3,4},{4,5},{5,6},{6,7},{7,8},{8,9},{9,10},{10,1... | collective-permute-start | bytes 6152 | tf_op jit(solution)/shard_map/ppermute | solution.py:15
  10.4 25.1 %all-to-all-start = ((bf16[488,8,64]{0,2,1:T(8,128)(2,1)}), bf16[488,8,64]{0,2,1:T(8,128)(2,1)S(1)}, u32[]{:S(2)}, u32[]{:S(2)}) async-start(bf16[488,8,64]{0,2,1:T(8,128)(2,1)} %bitcast.11), calls=%async_computation | async-start | bytes 1048576 | tf_op jit(solution)/shard_map/all_to_all | solution.py:39
  35.5 15.9 %collective-permute-start.2 = (bf16[488,512]{0,1:T(8,128)(2,1)S(1)}, bf16[488,512]{0,1:T(8,128)(2,1)S(1)}, u32[]{:S(2)}, u32[]{:S(2)}) collective-permute-start(bf16[488,512]{0,1:T(8,128)(2,1)S(1)} %bitcast.95), channel_id=1, source_target_pairs={{1,0},{2,1},{3,2},{4,3},{5,4},{6,5},{7,6},{8,7},{9,8},{10,9},{11,1... | collective-permute-start | bytes 1499144 | tf_op jit(solution)/shard_map/ppermute | solution.py:17
  39.5 15.6 %collective-permute-start = (bf16[488,512]{0,1:T(8,128)(2,1)S(1)}, bf16[488,512]{0,1:T(8,128)(2,1)S(1)}, u32[]{:S(2)}, u32[]{:S(2)}) collective-permute-start(bf16[488,512]{0,1:T(8,128)(2,1)S(1)} %bitcast.96), channel_id=1, source_target_pairs={{0,1},{1,2},{2,3},{3,4},{4,5},{5,6},{6,7},{7,8},{8,9},{9,10},{10,1... | collective-permute-start | bytes 1499144 | tf_op jit(solution)/shard_map/ppermute | solution.py:15
  74.9 4.1 %copy-start.1 = (bf16[8,488,488]{2,1,0:T(8,128)(2,1)S(1)}, bf16[8,488,488]{2,1,0:T(8,128)(2,1)}, u32[]{:S(2)}) copy-start(bf16[8,488,488]{2,1,0:T(8,128)(2,1)} %param.18) | copy-start | bytes 11430916
  74.9 4.1 %copy-start.3 = (bf16[512,488]{1,0:T(8,128)(2,1)S(1)}, bf16[512,488]{1,0:T(8,128)(2,1)}, u32[]{:S(2)}) copy-start(bf16[512,488]{1,0:T(8,128)(2,1)} %gather_fusion.5) | copy-start | bytes 1499140
  74.9 4.7 %copy-start.2 = (bf16[512,488]{1,0:T(8,128)(2,1)S(1)}, bf16[512,488]{1,0:T(8,128)(2,1)}, u32[]{:S(2)}) copy-start(bf16[512,488]{1,0:T(8,128)(2,1)} %gather_fusion.6) | copy-start | bytes 1499140
where the time goes:
time: 84.2 us; the launch traced here: 83.6 us
  starting transfers between devices  27 us (32%)
  local copies, waits for them, and re-layouts  24.8 us (29%)
  matrix products  12.4 us (15%)
  waiting for transfers between devices  12.2 us (14%)
  other arithmetic  6.74 us (8%)
    gather x8, local copies, waits for them, and re-layouts, body(): columns = jnp.take(sources, jnp.maximum(entries, 0), axis=1)  18.4 us
    all_to_all x1, starting transfers between devices, body(): lax.all_to_all(outgoing.reshape(coef_count, groups, capacity), 'grp', spl...  15 us
    ppermute x2, waiting for transfers between devices, extended(): lax.ppermute(head, axis, [((i + 1) % count, i) for i in range(ends)])  9.78 us
    dot_general x8, matrix products, body(): jnp.dot(m2l_ops[offset], columns, preferred_element_type=jnp.float32)  8.65 us
    ppermute x2, starting transfers between devices, extended(): lax.ppermute(head, axis, [((i + 1) % count, i) for i in range(ends)])  6.39 us
    ppermute x2, starting transfers between devices, extended(): lax.ppermute(tail, axis, [(i, (i + 1) % count) for i in range(ends)])  5.59 us
    dot_general x1, matrix products, body(): jnp.einsum('okj,jp->kop', l2l_ops, parent_local, preferred_element_type=j...  3.35 us
    gather x2, local copies, waits for them, and re-layouts, body(): accum_local = jnp.take(translated, parent_of, axis=1)  2.9 us
  transfers between devices with their start and end apart: 5, of which 2 were waited for; matrix products, arithmetic and copies ran while one was open for 19% of the time, Pallas kernels for 0%

commit v1 on v0

v1 whole, which is shorter than its diff:
```python
import functools

import jax
import jax.numpy as jnp
from jax import lax
from jax.experimental import pallas as pl
from jax.experimental.pallas import tpu as pltpu
from jax.sharding import PartitionSpec as P

MESH = pl.DeviceIdType.MESH
LANES = 128
F32 = jnp.float32
BF16 = jnp.bfloat16


def nt_dot(a, b):
    return lax.dot_general(a, b, (((1,), (1,)), ((), ())), preferred_element_type=F32)


def nn_dot(a, b):
    return jnp.dot(a, b, preferred_element_type=F32)


def iota(shape, dim):
    return lax.broadcasted_iota(jnp.int32, shape, dim)


def as_bf16(mask):
    return jnp.where(mask, jnp.ones((), F32), jnp.zeros((), F32)).astype(BF16)


def down_columns(row):
    return jnp.transpose(jnp.broadcast_to(row, (LANES, row.shape[1])))


def kernel(
    groups, columns, coef, boxes, slots, rim, parents, offsets, octants, chunks,
    mult_hbm, dest_hbm, par_hbm, pof_hbm, send_hbm, list_hbm, m2l_hbm, l2l_hbm,
    out_ref,
    mult, dest, par, pof, send, entries, m2l, l2l,
    outgoing, own, offer, near, hot, cols, blocks,
    in_sem, a_send, a_recv, n_send, n_recv,
):
    cap = slots // groups
    halves = chunks // 2
    g = lax.axis_index("grp")
    n = lax.axis_index("nbr")
    after = lax.rem(n + 1, columns)
    before = lax.rem(n + columns - 1, columns)

    loads = [
        pltpu.make_async_copy(src, dst, in_sem.at[i])
        for i, (src, dst) in enumerate(
            (
                (dest_hbm, dest),
                (mult_hbm, mult),
                (send_hbm, send),
                (list_hbm, entries),
                (par_hbm, par),
                (pof_hbm, pof),
                (l2l_hbm, l2l),
                (m2l_hbm, m2l),
            )
        )
    ]
    for load in loads:
        load.start()

    barrier = pltpu.get_barrier_semaphore()
    for d in range(1, groups):
        pl.semaphore_signal(
            barrier, inc=1, device_id=(lax.rem(g + d, groups), n), device_id_type=MESH
        )
    for to in (after, before):
        pl.semaphore_signal(barrier, inc=1, device_id=(g, to), device_id_type=MESH)

    loads[0].wait()
    owner = dest[...]
    named = iota((groups, boxes), 0) == owner
    earlier = as_bf16(iota((boxes, boxes), 0) < iota((boxes, boxes), 1))
    counts = nn_dot(as_bf16(named), earlier)
    arrival = jnp.sum(jnp.where(named, counts, jnp.zeros_like(counts)), axis=0, keepdims=True)
    position = owner * cap + arrival.astype(jnp.int32)
    placing = as_bf16(iota((slots, boxes), 0) == position)

    outgoing[chunks - 1] = jnp.zeros((slots, LANES), BF16)
    loads[1].wait()
    placed = nt_dot(placing, mult[...]).astype(BF16)
    for c in range(chunks):
        width = min(LANES, coef - c * LANES)
        outgoing[c, :, :width] = placed[:, c * LANES : c * LANES + width]
    mine = pl.ds(pl.multiple_of(g * cap, cap), cap)
    for c in range(chunks):
        own[c, mine, :] = outgoing[c, mine, :]

    def relay(c, d):
        to = lax.rem(g + d, groups)
        return pltpu.make_async_remote_copy(
            src_ref=outgoing.at[c, pl.ds(pl.multiple_of(to * cap, cap), cap)],
            dst_ref=own.at[c, mine],
            send_sem=a_send.at[c, d - 1],
            recv_sem=a_recv.at[c, d - 1],
            device_id=(to, n),
            device_id_type=MESH,
        )

    def hand(c, side):
        return pltpu.make_async_remote_copy(
            src_ref=offer.at[c, pl.ds(side * rim, rim)],
            dst_ref=near.at[c, pl.ds(side * rim, rim)],
            send_sem=n_send.at[c, side],
            recv_sem=n_recv.at[c, side],
            device_id=(g, (after, before)[side]),
            device_id_type=MESH,
        )

    pl.semaphore_wait(barrier, groups + 1)
    for c in range(chunks):
        for d in range(1, groups):
            relay(c, d).start()

    loads[2].wait()
    lane = iota((rim, LANES), 1)
    picks = []
    for side in range(2):
        wanted = down_columns(send[side : side + 1, :])
        picks.append(
            jnp.concatenate(
                [as_bf16(wanted == lane + t * LANES) for t in range(slots // LANES)], axis=1
            )
        )
    pick = jnp.concatenate(picks, axis=0)

    loads[3].wait()
    listed = entries[...]
    from_left = (listed >= slots) & (listed < slots + rim)
    from_right = listed >= slots + rim
    listed = jnp.where(from_left & (n == 0), -1, listed)
    entries[...] = jnp.where(from_right & (n == columns - 1), -1, listed)
    slot_lane = iota((slots, LANES), 1)

    def build(k):
        wanted = down_columns(entries[k : k + 1, :])
        for t in range(hot.shape[2] // LANES):
            hot[k, :, t * LANES : (t + 1) * LANES] = as_bf16(wanted == slot_lane + t * LANES)

    def pass_on(c):
        for d in range(1, groups):
            relay(c, d).wait_recv()
        offer[c] = nn_dot(pick, own[c]).astype(BF16)
        for side in range(2):
            hand(c, side).start()

    for k in range(offsets // 2):
        build(k)
    pass_on(0)
    for k in range(offsets // 2, offsets):
        build(k)
    pass_on(1)

    for i in (4, 5, 6):
        loads[i].wait()
    blocks[...] = jnp.zeros(blocks.shape, BF16)
    for q in range(octants):
        blocks[q, pl.ds(q * parents, parents), :] = par[...]
    translated = nt_dot(l2l[0], blocks[0])
    for q in range(1, octants):
        translated = translated + nt_dot(l2l[q], blocks[q])
    pass_on(2)
    upper = translated.astype(BF16)
    lower = (translated - upper.astype(F32)).astype(BF16)
    child = as_bf16(iota((octants * parents, slots), 0) == pof[...])
    out_ref[...] = nn_dot(upper, child) + nn_dot(lower, child)
    pass_on(3)

    def half_of(ref, h):
        return jnp.concatenate([ref[2 * h], ref[2 * h + 1]], axis=1)

    for h in range(halves):
        local = half_of(own, h)
        for k in range(offsets):
            cols[h, k] = nn_dot(hot[k, :, :slots], local).astype(BF16)

    loads[7].wait()
    for h in range(halves):
        for c in (2 * h, 2 * h + 1):
            for side in range(2):
                hand(c, side).wait_recv()
        beside = half_of(near, h)
        for k in range(offsets):
            cols[h, k] = cols[h, k] + nn_dot(hot[k, :, slots:], beside).astype(BF16)
        first = h * 2 * LANES
        width = min(2 * LANES, coef - first)
        total = out_ref[...]
        for k in range(offsets):
            total = total + nt_dot(m2l[k, :, first : first + width], cols[h, k, :, :width])
        out_ref[...] = total

    for c in range(chunks):
        for d in range(1, groups):
            relay(c, d).wait_send()
        for side in range(2):
            hand(c, side).wait_send()


def body(multipole, dest, parent_local, parent_of, send_list, lists, m2l_ops, l2l_ops):
    groups, columns = lax.axis_size("grp"), lax.axis_size("nbr")
    coef, boxes = multipole.shape
    offsets, slots = lists.shape
    octants = l2l_ops.shape[0]
    rim = send_list.shape[1]
    parents = parent_local.shape[1]
    chunks = -(-coef // LANES)
    dest_row = dest.reshape(1, boxes)
    parent_rows = parent_local.T
    child_row = parent_of.reshape(1, slots)
    args = (multipole, dest_row, parent_rows, child_row, send_list, lists, m2l_ops, l2l_ops)
    return pl.pallas_call(
        functools.partial(
            kernel, groups, columns, coef, boxes, slots, rim, parents, offsets, octants, chunks
        ),
        out_shape=jax.ShapeDtypeStruct((coef, slots), F32),
        in_specs=[pl.BlockSpec(memory_space=pl.ANY)] * len(args),
        out_specs=pl.BlockSpec(memory_space=pltpu.VMEM),
        scratch_shapes=[pltpu.VMEM(a.shape, a.dtype) for a in args]
        + [
            pltpu.VMEM((chunks, slots, LANES), BF16),
            pltpu.VMEM((chunks, slots, LANES), BF16),
            pltpu.VMEM((chunks, 2 * rim, LANES), BF16),
            pltpu.VMEM((chunks, 2 * rim, LANES), BF16),
            pltpu.VMEM((offsets, slots, slots + 2 * rim), BF16),
            pltpu.VMEM((chunks // 2, offsets, slots, 2 * LANES), BF16),
            pltpu.VMEM((octants, octants * parents, coef), BF16),
            pltpu.SemaphoreType.DMA((len(args),)),
            pltpu.SemaphoreType.DMA((chunks, groups - 1)),
            pltpu.SemaphoreType.DMA((chunks, groups - 1)),
            pltpu.SemaphoreType.DMA((chunks, 2)),
            pltpu.SemaphoreType.DMA((chunks, 2)),
        ],
        compiler_params=pltpu.CompilerParams(
            collective_id=0, has_side_effects=True, vmem_limit_bytes=48 * 1024 * 1024
        ),
        name="downward",
    )(*args)


def solution(mesh):
    placed = (
        P(None, ("grp", "nbr")),
        P(("grp", "nbr"), None),
        P(None, ("grp", "nbr")),
        P(("grp", "nbr")),
        P(None, ("grp", "nbr")),
        P(None, ("grp", "nbr")),
        P(),
        P(),
    )
    return jax.shard_map(
        body, mesh=mesh, in_specs=placed, out_specs=P(None, ("grp", "nbr")), check_vma=False
    )
```

time: 84.2 us -> 51.1 us (0.61)
  the two profiles are of different devices: /device:TPU:10 before, /device:TPU:1 now
where the time goes in v1:
time: 51.1 us; the launch traced here: 50.7 us
  Pallas kernels  43.1 us (84%)
  local copies, waits for them, and re-layouts  7.54 us (15%)
    pallas_call x1, Pallas kernels, body(): pl.pallas_call(functools.partial(kernel, groups, columns, coef, boxes, sl...  43.1 us
    unnamed x15, local copies, waits for them, and re-layouts  7.54 us

profile of v1, /device:TPU:1, one launch (start us, length us, event | category | flops | bytes accessed | tf_op | source)
XLA Modules:
  0.0 50.7 jit_solution(2649145330024189204)
XLA Ops:
  0.0 0.0 copy-start
  0.0 2.1 %copy-done = bf16[8,488,488]{2,1,0:T(8,128)(2,1)S(1)} copy-done((bf16[8,488,488]{2,1,0:T(8,128)(2,1)S(1)}, bf16[8,488,488]{2,1,0:T(8,128)(2,1)}, u32[]{:S(2)}) %copy-start) | copy-done | bytes 3810328
  2.1 0.0 copy-start.1
  2.1 0.9 %copy-done.1 = bf16[488,256]{1,0:T(8,128)(2,1)S(1)} copy-done((bf16[488,256]{1,0:T(8,128)(2,1)S(1)}, bf16[488,256]{1,0:T(8,128)(2,1)}, u32[]{:S(2)}) %copy-start.1) | copy-done | bytes 249880
  3.1 0.0 copy-start.2
  3.1 0.8 %copy-done.2 = bf16[488,32]{0,1:T(8,128)(2,1)S(1)} copy-done((bf16[488,32]{0,1:T(8,128)(2,1)S(1)}, bf16[488,32]{0,1:T(8,128)(2,1)}, u32[]{:S(2)}) %copy-start.2) | copy-done | bytes 31256
  3.8 0.0 copy-start.3
  3.8 0.7 %copy-done.3 = s32[8,512]{1,0:T(8,128)S(1)} copy-done((s32[8,512]{1,0:T(8,128)S(1)}, s32[8,512]{1,0:T(8,128)}, u32[]{:S(2)}) %copy-start.3) | copy-done | bytes 16408
  4.6 0.0 copy-start.4
  4.6 0.7 %copy-done.4 = s32[512]{0:T(512)S(1)} copy-done((s32[512]{0:T(512)S(1)}, s32[512]{0:T(512)}, u32[]{:S(2)}) %copy-start.4) | copy-done | bytes 2072
  5.2 0.0 copy-start.5
  5.2 0.7 %copy-done.5 = s32[2,256]{1,0:T(2,128)S(1)} copy-done((s32[2,256]{1,0:T(2,128)S(1)}, s32[2,256]{1,0:T(2,128)}, u32[]{:S(2)}) %copy-start.5) | copy-done | bytes 2072
  5.9 0.0 copy-start.6
  5.9 0.7 %copy-done.6 = s32[256,1]{0,1:T(1,128)S(1)} copy-done((s32[256,1]{0,1:T(1,128)S(1)}, s32[256,1]{0,1:T(1,128)}, u32[]{:S(2)}) %copy-start.6) | copy-done | bytes 1048
  6.6 43.1 %downward.1 = f32[488,512]{1,0:T(8,128)S(1)} custom-call(bf16[488,256]{1,0:T(8,128)(2,1)S(1)} %copy-done.1, s32[1,256]{1,0:T(1,128)S(1)} %bitcast.5, bf16[32,488]{1,0:T(8,128)(2,1)S(1)} %bitcast.3, s32[1,512]{1,0:T(1,128)S(1)} %bitcast.4, s32[2,256]{1,0:T(2,128)S(1)} %copy-done.5, s32[8,512]{1,0:T(8,128)S(1)} %copy-done.3, bf16[8,488,488]{2,1,0:T(8,128)(2,1)S(1)} %copy-done, ...), custom_call_target="tpu_custom_call" | custom-call | tf_op jit(solution)/shard_map/downward/pallas_call | solution.py:218
  49.7 1.0 %copy.10 = f32[488,512]{1,0:T(8,128)} copy(f32[488,512]{1,0:T(8,128)S(1)} %downward.1) | data formatting | bytes 1998848
Async XLA Ops:
  0.0 2.1 %copy-start = (bf16[8,488,488]{2,1,0:T(8,128)(2,1)S(1)}, bf16[8,488,488]{2,1,0:T(8,128)(2,1)}, u32[]{:S(2)}) copy-start(bf16[8,488,488]{2,1,0:T(8,128)(2,1)} %m2l_hbm.1) | copy-start | bytes 11430916
  2.1 0.9 %copy-start.1 = (bf16[488,256]{1,0:T(8,128)(2,1)S(1)}, bf16[488,256]{1,0:T(8,128)(2,1)}, u32[]{:S(2)}) copy-start(bf16[488,256]{1,0:T(8,128)(2,1)} %mult_hbm.1) | copy-start | bytes 749572
  3.1 0.8 %copy-start.2 = (bf16[488,32]{0,1:T(8,128)(2,1)S(1)}, bf16[488,32]{0,1:T(8,128)(2,1)}, u32[]{:S(2)}) copy-start(bf16[488,32]{0,1:T(8,128)(2,1)} %param.10) | copy-start | bytes 93700
  3.8 0.7 %copy-start.3 = (s32[8,512]{1,0:T(8,128)S(1)}, s32[8,512]{1,0:T(8,128)}, u32[]{:S(2)}) copy-start(s32[8,512]{1,0:T(8,128)} %list_hbm.1) | copy-start | bytes 49156
  4.6 0.7 %copy-start.4 = (s32[512]{0:T(512)S(1)}, s32[512]{0:T(512)}, u32[]{:S(2)}) copy-start(s32[512]{0:T(512)} %param.11) | copy-start | bytes 6148
  5.2 0.7 %copy-start.5 = (s32[2,256]{1,0:T(2,128)S(1)}, s32[2,256]{1,0:T(2,128)}, u32[]{:S(2)}) copy-start(s32[2,256]{1,0:T(2,128)} %send_hbm.1) | copy-start | bytes 6148
  5.9 0.7 %copy-start.6 = (s32[256,1]{0,1:T(1,128)S(1)}, s32[256,1]{0,1:T(1,128)}, u32[]{:S(2)}) copy-start(s32[256,1]{0,1:T(1,128)} %param.9) | copy-start | bytes 3076

commit v2 on v1

--- a/solution.py
+++ b/solution.py
@@ -39,14 +39,14 @@
     out_ref,
     mult, dest, par, pof, send, entries, m2l, l2l,
     outgoing, own, offer, near, hot, cols, blocks,
-    in_sem, a_send, a_recv, n_send, n_recv,
+    in_sem, a_send, a_recv, n_send, n_recv, group_in, columns_in,
 ):
     cap = slots // groups
     halves = chunks // 2
     g = lax.axis_index("grp")
     n = lax.axis_index("nbr")
-    after = lax.rem(n + 1, columns)
-    before = lax.rem(n + columns - 1, columns)
+    after, before = n + 1, n - 1
+    has_after, has_before = n < columns - 1, n > 0
 
     loads = [
         pltpu.make_async_copy(src, dst, in_sem.at[i])
@@ -67,12 +67,19 @@
         load.start()
 
     barrier = pltpu.get_barrier_semaphore()
-    for d in range(1, groups):
-        pl.semaphore_signal(
-            barrier, inc=1, device_id=(lax.rem(g + d, groups), n), device_id_type=MESH
-        )
-    for to in (after, before):
-        pl.semaphore_signal(barrier, inc=1, device_id=(g, to), device_id_type=MESH)
+
+    def tell(semaphore, member, column):
+        pl.semaphore_signal(semaphore, inc=1, device_id=(member, column), device_id_type=MESH)
+
+    @pl.when(g > 0)
+    def _():
+        tell(barrier, 0, n)
+
+    for has, to in ((has_after, after), (has_before, before)):
+
+        @pl.when(has)
+        def _():
+            tell(barrier, jnp.maximum(g, 1), to)
 
     loads[0].wait()
     owner = dest[...]
@@ -114,7 +121,16 @@
             device_id_type=MESH,
         )
 
-    pl.semaphore_wait(barrier, groups + 1)
+    @pl.when(g == 0)
+    def _():
+        pl.semaphore_wait(barrier, groups - 1)
+        for member in range(1, groups):
+            tell(group_in, member, n)
+
+    @pl.when(g > 0)
+    def _():
+        pl.semaphore_wait(group_in, 1)
+
     for c in range(chunks):
         for d in range(1, groups):
             relay(c, d).start()
@@ -144,19 +160,48 @@
         for t in range(hot.shape[2] // LANES):
             hot[k, :, t * LANES : (t + 1) * LANES] = as_bf16(wanted == slot_lane + t * LANES)
 
+    def know_columns():
+        ends = columns - 1
+        beside = (n + ends) // columns + (ends - n + ends) // columns
+
+        @pl.when(g > 1)
+        def _():
+            pl.semaphore_wait(barrier, beside)
+
+        @pl.when(g == 1)
+        def _():
+            pl.semaphore_wait(barrier, 2 * beside)
+
+        @pl.when(g == 1)
+        def _():
+            tell(columns_in, 0, n)
+
+        @pl.when(g == 0)
+        def _():
+            pl.semaphore_wait(columns_in, 1)
+
     def pass_on(c):
         for d in range(1, groups):
             relay(c, d).wait_recv()
         offer[c] = nn_dot(pick, own[c]).astype(BF16)
-        for side in range(2):
-            hand(c, side).start()
-
-    for k in range(offsets // 2):
+        if c == 0:
+            know_columns()
+        for side, has in enumerate((has_after, has_before)):
+
+            @pl.when(has)
+            def _():
+                hand(c, side).start()
+
+    def half_of(ref, h):
+        return jnp.concatenate([ref[2 * h], ref[2 * h + 1]], axis=1)
+
+    def from_own(h):
+        local = half_of(own, h)
+        for k in range(offsets):
+            cols[h, k] = nn_dot(hot[k, :, :slots], local).astype(BF16)
+
+    for k in range(offsets):
         build(k)
-    pass_on(0)
-    for k in range(offsets // 2, offsets):
-        build(k)
-    pass_on(1)
 
     for i in (4, 5, 6):
         loads[i].wait()
@@ -164,28 +209,41 @@
     for q in range(octants):
         blocks[q, pl.ds(q * parents, parents), :] = par[...]
     translated = nt_dot(l2l[0], blocks[0])
-    for q in range(1, octants):
+    for q in range(1, octants // 2):
         translated = translated + nt_dot(l2l[q], blocks[q])
-    pass_on(2)
+    out_ref[:, : octants * parents] = translated
+    pass_on(0)
+    translated = out_ref[:, : octants * parents]
+    for q in range(octants // 2, octants):
+        translated = translated + nt_dot(l2l[q], blocks[q])
     upper = translated.astype(BF16)
     lower = (translated - upper.astype(F32)).astype(BF16)
     child = as_bf16(iota((octants * parents, slots), 0) == pof[...])
     out_ref[...] = nn_dot(upper, child) + nn_dot(lower, child)
+    pass_on(1)
+    from_own(0)
+    pass_on(2)
     pass_on(3)
-
-    def half_of(ref, h):
-        return jnp.concatenate([ref[2 * h], ref[2 * h + 1]], axis=1)
-
-    for h in range(halves):
-        local = half_of(own, h)
-        for k in range(offsets):
-            cols[h, k] = nn_dot(hot[k, :, :slots], local).astype(BF16)
+    for h in range(1, halves):
+        from_own(h)
+
+    @pl.when(n == 0)
+    def _():
+        near[:, :rim] = jnp.zeros((chunks, rim, LANES), BF16)
+
+    @pl.when(n == columns - 1)
+    def _():
+        near[:, rim:] = jnp.zeros((chunks, rim, LANES), BF16)
 
     loads[7].wait()
     for h in range(halves):
         for c in (2 * h, 2 * h + 1):
-            for side in range(2):
-                hand(c, side).wait_recv()
+            for side, has in enumerate((has_before, has_after)):
+
+                @pl.when(has)
+                def _():
+                    hand(c, side).wait_recv()
+
         beside = half_of(near, h)
         for k in range(offsets):
             cols[h, k] = cols[h, k] + nn_dot(hot[k, :, slots:], beside).astype(BF16)
@@ -199,8 +257,11 @@
     for c in range(chunks):
         for d in range(1, groups):
             relay(c, d).wait_send()
-        for side in range(2):
-            hand(c, side).wait_send()
+        for side, has in enumerate((has_after, has_before)):
+
+            @pl.when(has)
+            def _():
+                hand(c, side).wait_send()
 
 
 def body(multipole, dest, parent_local, parent_of, send_list, lists, m2l_ops, l2l_ops):
@@ -214,13 +275,16 @@
     dest_row = dest.reshape(1, boxes)
     parent_rows = parent_local.T
     child_row = parent_of.reshape(1, slots)
-    args = (multipole, dest_row, parent_rows, child_row, send_list, lists, m2l_ops, l2l_ops)
+    args = [
+        pltpu.with_memory_space_constraint(a, pltpu.HBM)
+        for a in (multipole, dest_row, parent_rows, child_row, send_list, lists, m2l_ops, l2l_ops)
+    ]
     return pl.pallas_call(
         functools.partial(
             kernel, groups, columns, coef, boxes, slots, rim, parents, offsets, octants, chunks
         ),
         out_shape=jax.ShapeDtypeStruct((coef, slots), F32),
-        in_specs=[pl.BlockSpec(memory_space=pl.ANY)] * len(args),
+        in_specs=[pl.BlockSpec(memory_space=pltpu.HBM)] * len(args),
         out_specs=pl.BlockSpec(memory_space=pltpu.VMEM),
         scratch_shapes=[pltpu.VMEM(a.shape, a.dtype) for a in args]
         + [
@@ -236,6 +300,8 @@
             pltpu.SemaphoreType.DMA((chunks, groups - 1)),
             pltpu.SemaphoreType.DMA((chunks, 2)),
             pltpu.SemaphoreType.DMA((chunks, 2)),
+            pltpu.SemaphoreType.REGULAR,
+            pltpu.SemaphoreType.REGULAR,
         ],
         compiler_params=pltpu.CompilerParams(
             collective_id=0, has_side_effects=True, vmem_limit_bytes=48 * 1024 * 1024

time: 51.1 us -> 37.1 us (0.73)
  Pallas kernels: 43.1 us -> 36 us
  local copies, waits for them, and re-layouts: 7.54 us -> 0.95 us
    pallas_call x1, Pallas kernels: 43.1 us -> 36 us  [body(): pl.pallas_call(functools.partial(kernel, groups, columns, coef, boxes, sl...]
    unnamed x15 -> x1, local copies, waits for them, and re-layouts: 7.54 us -> 0.95 us
where the time goes in v2:
time: 37.1 us; the launch traced here: 37 us
  Pallas kernels  36 us (97%)
  local copies, waits for them, and re-layouts  0.95 us (3%)
    pallas_call x1, Pallas kernels, body(): pl.pallas_call(functools.partial(kernel, groups, columns, coef, boxes, sl...  36 us
    unnamed x1, local copies, waits for them, and re-layouts  0.95 us

profile of v2, /device:TPU:1, one launch (start us, length us, event | category | flops | bytes accessed | tf_op | source)
XLA Modules:
  0.0 37.0 jit_solution(6457758271448638232)
XLA Ops:
  0.0 36.0 %downward.1 = f32[488,512]{1,0:T(8,128)S(1)} custom-call(bf16[488,256]{1,0:T(8,128)(2,1)} %mult_hbm.1, s32[1,256]{1,0:T(1,128)} %bitcast.5, bf16[32,488]{1,0:T(8,128)(2,1)} %bitcast.3, s32[1,512]{1,0:T(1,128)} %bitcast.4, s32[2,256]{1,0:T(2,128)} %send_hbm.1, s32[8,512]{1,0:T(8,128)} %list_hbm.1, bf16[8,488,488]{2,1,0:T(8,128)(2,1)} %m2l_hbm.1, ...), custom_call_target="tpu_custom_call" | custom-call | tf_op jit(solution)/shard_map/downward/pallas_call | solution.py:282
  36.0 1.0 %copy.10 = f32[488,512]{1,0:T(8,128)} copy(f32[488,512]{1,0:T(8,128)S(1)} %downward.1) | data formatting | bytes 1998848

commit v3 on v2

--- a/solution.py
+++ b/solution.py
@@ -9,6 +9,8 @@
 
 MESH = pl.DeviceIdType.MESH
 LANES = 128
+WIDTH = 256
+HALF = 256
 F32 = jnp.float32
 BF16 = jnp.bfloat16
 
@@ -39,10 +41,11 @@
     out_ref,
     mult, dest, par, pof, send, entries, m2l, l2l,
     outgoing, own, offer, near, hot, cols, blocks,
-    in_sem, a_send, a_recv, n_send, n_recv, group_in, columns_in,
+    in_sem, a_send, a_recv, n_send, n_recv, group_in, first_in, columns_in,
 ):
     cap = slots // groups
-    halves = chunks // 2
+    per = HALF // WIDTH
+    halves = chunks // per
     g = lax.axis_index("grp")
     n = lax.axis_index("nbr")
     after, before = n + 1, n - 1
@@ -71,15 +74,19 @@
     def tell(semaphore, member, column):
         pl.semaphore_signal(semaphore, inc=1, device_id=(member, column), device_id_type=MESH)
 
-    @pl.when(g > 0)
-    def _():
-        tell(barrier, 0, n)
+    @pl.when(g == 0)
+    def _():
+        tell(barrier, 1, n)
+
+    @pl.when((g == 1) | (g > 2))
+    def _():
+        tell(barrier, 2, n)
 
     for has, to in ((has_after, after), (has_before, before)):
 
         @pl.when(has)
         def _():
-            tell(barrier, jnp.maximum(g, 1), to)
+            tell(barrier, jnp.where((g == 1) | (g == 2), g + 2, g), to)
 
     loads[0].wait()
     owner = dest[...]
@@ -90,12 +97,12 @@
     position = owner * cap + arrival.astype(jnp.int32)
     placing = as_bf16(iota((slots, boxes), 0) == position)
 
-    outgoing[chunks - 1] = jnp.zeros((slots, LANES), BF16)
+    outgoing[chunks - 1] = jnp.zeros((slots, WIDTH), BF16)
     loads[1].wait()
     placed = nt_dot(placing, mult[...]).astype(BF16)
     for c in range(chunks):
-        width = min(LANES, coef - c * LANES)
-        outgoing[c, :, :width] = placed[:, c * LANES : c * LANES + width]
+        width = min(WIDTH, coef - c * WIDTH)
+        outgoing[c, :, :width] = placed[:, c * WIDTH : c * WIDTH + width]
     mine = pl.ds(pl.multiple_of(g * cap, cap), cap)
     for c in range(chunks):
         own[c, mine, :] = outgoing[c, mine, :]
@@ -120,20 +127,6 @@
             device_id=(g, (after, before)[side]),
             device_id_type=MESH,
         )
-
-    @pl.when(g == 0)
-    def _():
-        pl.semaphore_wait(barrier, groups - 1)
-        for member in range(1, groups):
-            tell(group_in, member, n)
-
-    @pl.when(g > 0)
-    def _():
-        pl.semaphore_wait(group_in, 1)
-
-    for c in range(chunks):
-        for d in range(1, groups):
-            relay(c, d).start()
 
     loads[2].wait()
     lane = iota((rim, LANES), 1)
@@ -164,19 +157,16 @@
         ends = columns - 1
         beside = (n + ends) // columns + (ends - n + ends) // columns
 
-        @pl.when(g > 1)
+        @pl.when((g == 0) | (g > 4))
         def _():
             pl.semaphore_wait(barrier, beside)
 
-        @pl.when(g == 1)
+        @pl.when((g == 3) | (g == 4))
         def _():
             pl.semaphore_wait(barrier, 2 * beside)
-
-        @pl.when(g == 1)
-        def _():
-            tell(columns_in, 0, n)
-
-        @pl.when(g == 0)
+            tell(columns_in, g - 2, n)
+
+        @pl.when((g == 1) | (g == 2))
         def _():
             pl.semaphore_wait(columns_in, 1)
 
@@ -193,7 +183,7 @@
                 hand(c, side).start()
 
     def half_of(ref, h):
-        return jnp.concatenate([ref[2 * h], ref[2 * h + 1]], axis=1)
+        return jnp.concatenate([ref[per * h + i] for i in range(per)], axis=1)
 
     def from_own(h):
         local = half_of(own, h)
@@ -202,6 +192,42 @@
 
     for k in range(offsets):
         build(k)
+
+    @pl.when(g == 2)
+    def _():
+        pl.semaphore_wait(barrier, groups - 2)
+        for member in range(1, groups):
+            if member != 2:
+                tell(group_in, member, n)
+
+    @pl.when((g == 1) | (g > 2))
+    def _():
+        pl.semaphore_wait(group_in, 1)
+
+    for c in range(chunks):
+        for d in range(1, groups):
+
+            @pl.when((g > 0) & (g + d != groups))
+            def _():
+                relay(c, d).start()
+
+    @pl.when(g == 1)
+    def _():
+        pl.semaphore_wait(barrier, 1)
+        for member in range(groups):
+            if member != 1:
+                tell(first_in, member, n)
+
+    @pl.when(g != 1)
+    def _():
+        pl.semaphore_wait(first_in, 1)
+
+    for c in range(chunks):
+        for d in range(1, groups):
+
+            @pl.when((g == 0) | (g + d == groups))
+            def _():
+                relay(c, d).start()
 
     for i in (4, 5, 6):
         loads[i].wait()
@@ -209,35 +235,28 @@
     for q in range(octants):
         blocks[q, pl.ds(q * parents, parents), :] = par[...]
     translated = nt_dot(l2l[0], blocks[0])
-    for q in range(1, octants // 2):
-        translated = translated + nt_dot(l2l[q], blocks[q])
-    out_ref[:, : octants * parents] = translated
-    pass_on(0)
-    translated = out_ref[:, : octants * parents]
-    for q in range(octants // 2, octants):
+    for q in range(1, octants):
         translated = translated + nt_dot(l2l[q], blocks[q])
     upper = translated.astype(BF16)
     lower = (translated - upper.astype(F32)).astype(BF16)
     child = as_bf16(iota((octants * parents, slots), 0) == pof[...])
     out_ref[...] = nn_dot(upper, child) + nn_dot(lower, child)
-    pass_on(1)
-    from_own(0)
-    pass_on(2)
-    pass_on(3)
-    for h in range(1, halves):
+    for h in range(halves):
+        for c in range(per * h, per * h + per):
+            pass_on(c)
         from_own(h)
 
     @pl.when(n == 0)
     def _():
-        near[:, :rim] = jnp.zeros((chunks, rim, LANES), BF16)
+        near[:, :rim] = jnp.zeros((chunks, rim, WIDTH), BF16)
 
     @pl.when(n == columns - 1)
     def _():
-        near[:, rim:] = jnp.zeros((chunks, rim, LANES), BF16)
+        near[:, rim:] = jnp.zeros((chunks, rim, WIDTH), BF16)
 
     loads[7].wait()
     for h in range(halves):
-        for c in (2 * h, 2 * h + 1):
+        for c in range(per * h, per * h + per):
             for side, has in enumerate((has_before, has_after)):
 
                 @pl.when(has)
@@ -247,8 +266,8 @@
         beside = half_of(near, h)
         for k in range(offsets):
             cols[h, k] = cols[h, k] + nn_dot(hot[k, :, slots:], beside).astype(BF16)
-        first = h * 2 * LANES
-        width = min(2 * LANES, coef - first)
+        first = h * HALF
+        width = min(HALF, coef - first)
         total = out_ref[...]
         for k in range(offsets):
             total = total + nt_dot(m2l[k, :, first : first + width], cols[h, k, :, :width])
@@ -271,7 +290,7 @@
     octants = l2l_ops.shape[0]
     rim = send_list.shape[1]
     parents = parent_local.shape[1]
-    chunks = -(-coef // LANES)
+    chunks = -(-coef // HALF) * (HALF // WIDTH)
     dest_row = dest.reshape(1, boxes)
     parent_rows = parent_local.T
     child_row = parent_of.reshape(1, slots)
@@ -288,18 +307,19 @@
         out_specs=pl.BlockSpec(memory_space=pltpu.VMEM),
         scratch_shapes=[pltpu.VMEM(a.shape, a.dtype) for a in args]
         + [
-            pltpu.VMEM((chunks, slots, LANES), BF16),
-            pltpu.VMEM((chunks, slots, LANES), BF16),
-            pltpu.VMEM((chunks, 2 * rim, LANES), BF16),
-            pltpu.VMEM((chunks, 2 * rim, LANES), BF16),
+            pltpu.VMEM((chunks, slots, WIDTH), BF16),
+            pltpu.VMEM((chunks, slots, WIDTH), BF16),
+            pltpu.VMEM((chunks, 2 * rim, WIDTH), BF16),
+            pltpu.VMEM((chunks, 2 * rim, WIDTH), BF16),
             pltpu.VMEM((offsets, slots, slots + 2 * rim), BF16),
-            pltpu.VMEM((chunks // 2, offsets, slots, 2 * LANES), BF16),
+            pltpu.VMEM((-(-coef // HALF), offsets, slots, HALF), BF16),
             pltpu.VMEM((octants, octants * parents, coef), BF16),
             pltpu.SemaphoreType.DMA((len(args),)),
             pltpu.SemaphoreType.DMA((chunks, groups - 1)),
             pltpu.SemaphoreType.DMA((chunks, groups - 1)),
             pltpu.SemaphoreType.DMA((chunks, 2)),
             pltpu.SemaphoreType.DMA((chunks, 2)),
+            pltpu.SemaphoreType.REGULAR,
             pltpu.SemaphoreType.REGULAR,
             pltpu.SemaphoreType.REGULAR,
         ],

time: 37.1 us -> 32.9 us (0.89)
  the two profiles are of different devices: /device:TPU:1 before, /device:TPU:10 now
where the time goes in v3:
time: 32.9 us; the launch traced here: 32.7 us
  Pallas kernels  31.8 us (97%)
  local copies, waits for them, and re-layouts  0.95 us (3%)
    pallas_call x1, Pallas kernels, body(): pl.pallas_call(functools.partial(kernel, groups, columns, coef, boxes, sl...  31.8 us
    unnamed x1, local copies, waits for them, and re-layouts  0.95 us

profile of v3, /device:TPU:10, one launch (start us, length us, event | category | flops | bytes accessed | tf_op | source)
XLA Modules:
  0.0 32.7 jit_solution(5101030125590733471)
XLA Ops:
  0.0 31.8 %downward.1 = f32[488,512]{1,0:T(8,128)S(1)} custom-call(bf16[488,256]{1,0:T(8,128)(2,1)} %mult_hbm.1, s32[1,256]{1,0:T(1,128)} %bitcast.5, bf16[32,488]{1,0:T(8,128)(2,1)} %bitcast.3, s32[1,512]{1,0:T(1,128)} %bitcast.4, s32[2,256]{1,0:T(2,128)} %send_hbm.1, s32[8,512]{1,0:T(8,128)} %list_hbm.1, bf16[8,488,488]{2,1,0:T(8,128)(2,1)} %m2l_hbm.1, ...), custom_call_target="tpu_custom_call" | custom-call | tf_op jit(solution)/shard_map/downward/pallas_call | solution.py:301
  31.8 1.0 %copy.10 = f32[488,512]{1,0:T(8,128)} copy(f32[488,512]{1,0:T(8,128)S(1)} %downward.1) | data formatting | bytes 1998848

commit v4 on v3

--- a/solution.py
+++ b/solution.py
@@ -50,6 +50,7 @@
     n = lax.axis_index("nbr")
     after, before = n + 1, n - 1
     has_after, has_before = n < columns - 1, n > 0
+    apart = n == 0
 
     loads = [
         pltpu.make_async_copy(src, dst, in_sem.at[i])
@@ -76,7 +77,7 @@
 
     @pl.when(g == 0)
     def _():
-        tell(barrier, 1, n)
+        tell(barrier, jnp.where(apart, 1, 2), n)
 
     @pl.when((g == 1) | (g > 2))
     def _():
@@ -190,44 +191,40 @@
         for k in range(offsets):
             cols[h, k] = nn_dot(hot[k, :, :slots], local).astype(BF16)
 
-    for k in range(offsets):
-        build(k)
-
-    @pl.when(g == 2)
+    @pl.when((g == 2) & apart)
     def _():
         pl.semaphore_wait(barrier, groups - 2)
         for member in range(1, groups):
             if member != 2:
                 tell(group_in, member, n)
 
-    @pl.when((g == 1) | (g > 2))
+    @pl.when((g == 2) & (n > 0))
+    def _():
+        pl.semaphore_wait(barrier, groups - 1)
+        for member in range(groups):
+            if member != 2:
+                tell(group_in, member, n)
+
+    @pl.when((g == 1) | (g > 2) | ((g == 0) & (n > 0)))
     def _():
         pl.semaphore_wait(group_in, 1)
 
     for c in range(chunks):
         for d in range(1, groups):
 
-            @pl.when((g > 0) & (g + d != groups))
+            @pl.when((n > 0) | ((g > 0) & (g + d != groups)))
             def _():
                 relay(c, d).start()
 
-    @pl.when(g == 1)
-    def _():
-        pl.semaphore_wait(barrier, 1)
-        for member in range(groups):
-            if member != 1:
-                tell(first_in, member, n)
-
-    @pl.when(g != 1)
+    @pl.when((g == 0) & apart)
     def _():
         pl.semaphore_wait(first_in, 1)
-
-    for c in range(chunks):
-        for d in range(1, groups):
-
-            @pl.when((g == 0) | (g + d == groups))
-            def _():
+        for c in range(chunks):
+            for d in range(1, groups):
                 relay(c, d).start()
+
+    for k in range(offsets):
+        build(k)
 
     for i in (4, 5, 6):
         loads[i].wait()
@@ -241,6 +238,22 @@
     lower = (translated - upper.astype(F32)).astype(BF16)
     child = as_bf16(iota((octants * parents, slots), 0) == pof[...])
     out_ref[...] = nn_dot(upper, child) + nn_dot(lower, child)
+    @pl.when((g == 1) & apart)
+    def _():
+        pl.semaphore_wait(barrier, 1)
+        for member in range(groups):
+            if member != 1:
+                tell(first_in, member, n)
+
+    @pl.when((g > 1) & apart)
+    def _():
+        pl.semaphore_wait(first_in, 1)
+
+    @pl.when((g > 0) & apart)
+    def _():
+        for c in range(chunks):
+            relay(c, groups - g).start()
+
     for h in range(halves):
         for c in range(per * h, per * h + per):
             pass_on(c)

time: 32.9 us -> 31.2 us (0.948)
  the two profiles are of different devices: /device:TPU:10 before, /device:TPU:8 now
where the time goes in v4:
time: 31.2 us; the launch traced here: 31 us
  Pallas kernels  30.1 us (96%)
  local copies, waits for them, and re-layouts  0.95 us (3%)
    pallas_call x1, Pallas kernels, body(): pl.pallas_call(functools.partial(kernel, groups, columns, coef, boxes, sl...  30.1 us
    unnamed x1, local copies, waits for them, and re-layouts  0.95 us

profile of v4, /device:TPU:8, one launch (start us, length us, event | category | flops | bytes accessed | tf_op | source)
XLA Modules:
  0.0 31.0 jit_solution(2510589750639187038)
XLA Ops:
  0.0 30.1 %downward.1 = f32[488,512]{1,0:T(8,128)S(1)} custom-call(bf16[488,256]{1,0:T(8,128)(2,1)} %mult_hbm.1, s32[1,256]{1,0:T(1,128)} %bitcast.5, bf16[32,488]{1,0:T(8,128)(2,1)} %bitcast.3, s32[1,512]{1,0:T(1,128)} %bitcast.4, s32[2,256]{1,0:T(2,128)} %send_hbm.1, s32[8,512]{1,0:T(8,128)} %list_hbm.1, bf16[8,488,488]{2,1,0:T(8,128)(2,1)} %m2l_hbm.1, ...), custom_call_target="tpu_custom_call" | custom-call | tf_op jit(solution)/shard_map/downward/pallas_call | solution.py:314
  30.1 1.0 %copy.10 = f32[488,512]{1,0:T(8,128)} copy(f32[488,512]{1,0:T(8,128)S(1)} %downward.1) | data formatting | bytes 1998848

commit v5 on v4

--- a/solution.py
+++ b/solution.py
@@ -41,14 +41,14 @@
     out_ref,
     mult, dest, par, pof, send, entries, m2l, l2l,
     outgoing, own, offer, near, hot, cols, blocks,
-    in_sem, a_send, a_recv, n_send, n_recv, group_in, first_in, columns_in,
+    in_sem, a_send, a_recv, n_send, n_recv, group_in, first_in, before_in, after_in,
 ):
     cap = slots // groups
     per = HALF // WIDTH
     halves = chunks // per
     g = lax.axis_index("grp")
     n = lax.axis_index("nbr")
-    after, before = n + 1, n - 1
+    after, before = lax.rem(n + 1, columns), lax.rem(n + columns - 1, columns)
     has_after, has_before = n < columns - 1, n > 0
     apart = n == 0
 
@@ -75,19 +75,26 @@
     def tell(semaphore, member, column):
         pl.semaphore_signal(semaphore, inc=1, device_id=(member, column), device_id_type=MESH)
 
-    @pl.when(g == 0)
-    def _():
-        tell(barrier, jnp.where(apart, 1, 2), n)
-
-    @pl.when((g == 1) | (g > 2))
+    for d in range(1, groups):
+        member = lax.rem(g + d, groups)
+
+        @pl.when((n > 0) & (member != 0) & (member != 4))
+        def _():
+            tell(barrier, member, n)
+
+    @pl.when((g == 0) & apart)
+    def _():
+        tell(barrier, 1, n)
+
+    @pl.when(((g == 1) | (g > 2)) & apart)
     def _():
         tell(barrier, 2, n)
 
-    for has, to in ((has_after, after), (has_before, before)):
+    for has, to, member in ((has_after, after, 0), (has_before, before, 4)):
 
         @pl.when(has)
         def _():
-            tell(barrier, jnp.where((g == 1) | (g == 2), g + 2, g), to)
+            tell(barrier, member, to)
 
     loads[0].wait()
     owner = dest[...]
@@ -154,30 +161,30 @@
         for t in range(hot.shape[2] // LANES):
             hot[k, :, t * LANES : (t + 1) * LANES] = as_bf16(wanted == slot_lane + t * LANES)
 
-    def know_columns():
-        ends = columns - 1
-        beside = (n + ends) // columns + (ends - n + ends) // columns
-
-        @pl.when((g == 0) | (g > 4))
+    sides = ((1, has_before, 0, before_in), (0, has_after, 4, after_in))
+
+    def hear_columns():
+        for _, has, listener, semaphore in sides:
+
+            @pl.when((g == listener) & has)
+            def _():
+                pl.semaphore_wait(barrier, groups)
+                for member in range(groups):
+                    if member != listener:
+                        tell(semaphore, member, n)
+
+    def know_column(has, listener, semaphore):
+        @pl.when((g != listener) & has)
         def _():
-            pl.semaphore_wait(barrier, beside)
-
-        @pl.when((g == 3) | (g == 4))
-        def _():
-            pl.semaphore_wait(barrier, 2 * beside)
-            tell(columns_in, g - 2, n)
-
-        @pl.when((g == 1) | (g == 2))
-        def _():
-            pl.semaphore_wait(columns_in, 1)
+            pl.semaphore_wait(semaphore, 1)
 
     def pass_on(c):
         for d in range(1, groups):
             relay(c, d).wait_recv()
         offer[c] = nn_dot(pick, own[c]).astype(BF16)
-        if c == 0:
-            know_columns()
-        for side, has in enumerate((has_after, has_before)):
+        for side, has, listener, semaphore in sides:
+            if c == 0:
+                know_column(has, listener, semaphore)
 
             @pl.when(has)
             def _():
@@ -198,14 +205,19 @@
             if member != 2:
                 tell(group_in, member, n)
 
-    @pl.when((g == 2) & (n > 0))
+    @pl.when((g != 0) & (g != 4) & (n > 0))
     def _():
         pl.semaphore_wait(barrier, groups - 1)
-        for member in range(groups):
-            if member != 2:
-                tell(group_in, member, n)
-
-    @pl.when((g == 1) | (g > 2) | ((g == 0) & (n > 0)))
+
+    @pl.when(((g == 1) | (g == 5)) & (n > 0))
+    def _():
+        tell(group_in, g - 1, n)
+
+    @pl.when(((g == 0) | (g == 4)) & (n > 0))
+    def _():
+        pl.semaphore_wait(group_in, 1)
+
+    @pl.when(((g == 1) | (g > 2)) & apart)
     def _():
         pl.semaphore_wait(group_in, 1)
 
@@ -254,6 +266,7 @@
         for c in range(chunks):
             relay(c, groups - g).start()
 
+    hear_columns()
     for h in range(halves):
         for c in range(per * h, per * h + per):
             pass_on(c)
@@ -335,6 +348,7 @@
             pltpu.SemaphoreType.REGULAR,
             pltpu.SemaphoreType.REGULAR,
             pltpu.SemaphoreType.REGULAR,
+            pltpu.SemaphoreType.REGULAR,
         ],
         compiler_params=pltpu.CompilerParams(
             collective_id=0, has_side_effects=True, vmem_limit_bytes=48 * 1024 * 1024

time: 31.2 us -> 30.2 us (0.968)
  Pallas kernels: 30.1 us -> 29.1 us
    pallas_call x1, Pallas kernels: 30.1 us -> 29.1 us  [body(): pl.pallas_call(functools.partial(kernel, groups, columns, coef, boxes, sl...]
where the time goes in v5:
time: 30.2 us; the launch traced here: 30.1 us
  Pallas kernels  29.1 us (96%)
  local copies, waits for them, and re-layouts  0.95 us (3%)
    pallas_call x1, Pallas kernels, body(): pl.pallas_call(functools.partial(kernel, groups, columns, coef, boxes, sl...  29.1 us
    unnamed x1, local copies, waits for them, and re-layouts  0.95 us

profile of v5, /device:TPU:8, one launch (start us, length us, event | category | flops | bytes accessed | tf_op | source)
XLA Modules:
  0.0 30.1 jit_solution(3589473122339983127)
XLA Ops:
  0.0 29.1 %downward.1 = f32[488,512]{1,0:T(8,128)S(1)} custom-call(bf16[488,256]{1,0:T(8,128)(2,1)} %mult_hbm.1, s32[1,256]{1,0:T(1,128)} %bitcast.5, bf16[32,488]{1,0:T(8,128)(2,1)} %bitcast.3, s32[1,512]{1,0:T(1,128)} %bitcast.4, s32[2,256]{1,0:T(2,128)} %send_hbm.1, s32[8,512]{1,0:T(8,128)} %list_hbm.1, bf16[8,488,488]{2,1,0:T(8,128)(2,1)} %m2l_hbm.1, ...), custom_call_target="tpu_custom_call" | custom-call | tf_op jit(solution)/shard_map/downward/pallas_call | solution.py:327
  29.1 1.0 %copy.10 = f32[488,512]{1,0:T(8,128)} copy(f32[488,512]{1,0:T(8,128)S(1)} %downward.1) | data formatting | bytes 1998848

commit v6 on v5

--- a/solution.py
+++ b/solution.py
@@ -267,9 +267,9 @@
             relay(c, groups - g).start()
 
     hear_columns()
+    for c in range(chunks):
+        pass_on(c)
     for h in range(halves):
-        for c in range(per * h, per * h + per):
-            pass_on(c)
         from_own(h)
 
     @pl.when(n == 0)

time: 30.2 us -> 30.2 us (level)
  no operation moved by 1% of the time
where the time goes in v6:
time: 30.2 us; the launch traced here: 30.1 us
  Pallas kernels  29.1 us (96%)
  local copies, waits for them, and re-layouts  0.95 us (3%)
    pallas_call x1, Pallas kernels, body(): pl.pallas_call(functools.partial(kernel, groups, columns, coef, boxes, sl...  29.1 us
    unnamed x1, local copies, waits for them, and re-layouts  0.95 us

profile of v6, /device:TPU:8, one launch (start us, length us, event | category | flops | bytes accessed | tf_op | source)
XLA Modules:
  0.0 30.1 jit_solution(18067502733939384164)
XLA Ops:
  0.0 29.1 %downward.1 = f32[488,512]{1,0:T(8,128)S(1)} custom-call(bf16[488,256]{1,0:T(8,128)(2,1)} %mult_hbm.1, s32[1,256]{1,0:T(1,128)} %bitcast.5, bf16[32,488]{1,0:T(8,128)(2,1)} %bitcast.3, s32[1,512]{1,0:T(1,128)} %bitcast.4, s32[2,256]{1,0:T(2,128)} %send_hbm.1, s32[8,512]{1,0:T(8,128)} %list_hbm.1, bf16[8,488,488]{2,1,0:T(8,128)(2,1)} %m2l_hbm.1, ...), custom_call_target="tpu_custom_call" | custom-call | tf_op jit(solution)/shard_map/downward/pallas_call | solution.py:327
  29.1 1.0 %copy.10 = f32[488,512]{1,0:T(8,128)} copy(f32[488,512]{1,0:T(8,128)S(1)} %downward.1) | data formatting | bytes 1998848
